TPU v7x, 32 devices: a whole 2x2x4 slice. The times are simulated.
32 devices in a mesh: ctx: 16 (over z, x, core), exp: 2 (over y).
Axes of the slice: x: 2, y: 2, z: 4, core: 2. Of those that a mesh axis runs over, the one named last changes fastest.
Arguments:
- hidden_in: bfloat16 [4096, 2048], P(('ctx', 'exp')), may hold values from -6 to 6
- queries: bfloat16 [4096, 4096], P('ctx', 'exp'), may hold values from -400 to 400
- keys: bfloat16 [4096, 512], P('ctx'), may hold values from -8 to 8
- values: bfloat16 [4096, 512], P('ctx'), may hold values from -6 to 6
- blocks: int32 [32, 8], P('ctx'), may hold values from 0 to 31, as said below
- out_weight: bfloat16 [4096, 2048], P('exp'), may hold values from -0.75 to 0.75
- norm_gain: float32 [2048], replicated, may hold values from 0.1 to 1.9
- w_gate_up: bfloat16 [8, 2048, 1536], P('exp'), may hold values from -0.125 to 0.125
- w_down: bfloat16 [8, 768, 2048], P('exp'), may hold values from -0.21875 to 0.21875
- expert_ids: int32 [4096, 2], P(('ctx', 'exp')), may hold values from 0 to 7, all different within a row; in each aligned block of 128 rows (0 to 127, 128 to 255, ...) at most 64 rows name the same one
- gate_weights: float32 [4096, 2], P(('ctx', 'exp')), may hold values from 0.25 to 1
Outputs:
- layer_out: bfloat16 [4096, 2048], P(('ctx', 'exp'))
Inputs may be any that keep to these rules, and one draw needn't show every extreme that they name: Row b lists key blocks for query block b: its first entry is b, every entry lies in 0 to b, and entries may repeat. `expert_ids`: A token's 2 experts are distinct. Within the 128 rows of one device (aligned blocks of rows), no expert is named more than 64 times, a bound that some block reaches.
All inputs are finite; a program needn't handle non-finite values.
Results may differ from a plain program's by a relative error of at most 0.019.
Values may be sent and summed in bfloat16 or wider, within the bound.
A program may use at most 128 MiB of HBM per device.

v0:
```python
import math

import jax
import jax.numpy as jnp
from jax import lax
from jax.sharding import PartitionSpec as P

HQ = 32
KVH = 4
HD = 128
FF = 768
BLK = 128


NEG_FILL = -1e30


def shifted(value, axis, steps):
    count = lax.axis_size(axis)
    first, last = (max(0, -steps), min(count, count - steps))
    return lax.ppermute(value, axis, [(source, source + steps) for source in range(first, last)])


def body(
    hidden_in,
    queries,
    keys,
    values,
    blocks,
    out_weight,
    norm_gain,
    w_gate_up,
    w_down,
    expert_ids,
    gate_weights,
):
    query_len = queries.shape[0]
    local_heads = queries.shape[1] // HD
    head_group = HQ // KVH
    local_group = min(head_group, local_heads)
    kv_local = local_heads // local_group
    kv_width = kv_local * HD
    first_kv = lax.axis_index("exp") * local_heads // head_group
    kv_mine = jnp.concatenate(
        [
            lax.dynamic_slice_in_dim(keys, first_kv * HD, kv_width, 1),
            lax.dynamic_slice_in_dim(values, first_kv * HD, kv_width, 1),
        ],
        axis=1,
    )
    cycle_size = lax.axis_size("ctx")
    ctx_place = lax.axis_index("ctx")
    query_start = ctx_place * query_len
    score_scale = 1.0 / math.sqrt(HD)
    query_heads = queries.reshape(query_len, kv_local, local_group, HD)
    query_pos = query_start + jnp.arange(query_len, dtype=jnp.int32)
    query_tiles = blocks.shape[0]

    def update(state, key_part, value_part, live):
        running_max, weight_sum, accumulated = state
        row_count = key_part.shape[0]
        scores = (
            jnp.einsum(
                "skgd,tkd->skgt",
                query_heads,
                key_part.reshape(row_count, kv_local, HD),
                preferred_element_type=jnp.float32,
            )
            * score_scale
        )
        live_full = live[:, None, None, :]
        new_max = jnp.maximum(running_max, jnp.max(jnp.where(live_full, scores, NEG_FILL), axis=-1))
        weights = jnp.where(live_full, jnp.exp(scores - new_max[..., None]), 0.0)
        shrink = jnp.exp(running_max - new_max)
        weight_sum = weight_sum * shrink + jnp.sum(weights, axis=-1)
        product = jnp.einsum(
            "skgt,tkd->skgd",
            weights.astype(jnp.bfloat16),
            value_part.reshape(row_count, kv_local, HD),
            preferred_element_type=jnp.float32,
        )
        accumulated = accumulated * shrink[..., None] + product
        return (new_max, weight_sum, accumulated)

    def attend_block(state, kv_part, row_start):
        row_count = kv_part.shape[0]
        key_part = kv_part[:, :kv_width]
        value_part = kv_part[:, kv_width:]
        key_pos = row_start + jnp.arange(row_count, dtype=jnp.int32)
        listed = jnp.any(blocks[:, :, None] == (key_pos // BLK)[None, None, :], axis=1)
        listed_rows = jnp.broadcast_to(listed[:, None, :], (query_tiles, BLK, row_count)).reshape(
            query_len, row_count
        )
        live = listed_rows & (key_pos[None, :] <= query_pos[:, None])
        result_state = update(state, key_part, value_part, live)
        return result_state

    def attend(state, kv_part, row_start):
        row_count = kv_part.shape[0]
        return attend_block(state, kv_part, row_start)

    empty_state = (
        jnp.full((query_len, kv_local, local_group), NEG_FILL, jnp.float32),
        jnp.zeros((query_len, kv_local, local_group), jnp.float32),
        jnp.zeros((query_len, kv_local, local_group, HD), jnp.float32),
    )
    first_state = attend(empty_state, kv_mine, query_start)

    def cycle_turn(turn, carried):
        acc_state, travelling = carried
        travelling = shifted(travelling, "ctx", 1)
        source = (ctx_place - turn - 1) % cycle_size
        return (attend(acc_state, travelling, source * query_len), travelling)

    final_state, unused_kv = lax.fori_loop(0, cycle_size - 1, cycle_turn, (first_state, kv_mine))
    running_max, weight_sum, accumulated = final_state
    attended = (
        (accumulated / weight_sum[..., None])
        .astype(jnp.bfloat16)
        .reshape(query_len, local_heads * HD)
    )
    token_count = hidden_in.shape[0]
    mixed = lax.psum_scatter(
        jnp.dot(attended, out_weight, preferred_element_type=jnp.float32).astype(jnp.bfloat16),
        "exp",
        scatter_dimension=0,
        tiled=True,
    ).astype(jnp.float32)
    hidden = (hidden_in.astype(jnp.float32) + mixed).astype(jnp.bfloat16)
    hidden_f = lax.optimization_barrier(hidden).astype(jnp.float32)
    mean_square = jnp.mean(hidden_f * hidden_f, axis=-1, keepdims=True)
    normed = (hidden_f * lax.rsqrt(mean_square + 1e-06) * norm_gain).astype(jnp.bfloat16)
    exp_size = lax.axis_size("exp")
    local_experts = w_gate_up.shape[0]
    expert_total = local_experts * exp_size
    capacity = token_count // 2
    model_width = normed.shape[1]
    route_count = expert_ids.shape[1]
    flat_ids = expert_ids.reshape(token_count * route_count)
    onehot = (flat_ids[:, None] == jnp.arange(expert_total, dtype=jnp.int32)[None, :]).astype(
        jnp.int32
    )
    slot_rank = jnp.sum((jnp.cumsum(onehot, axis=0) - onehot) * onehot, axis=1)
    target = (flat_ids * capacity + slot_rank).reshape(token_count, route_count)
    slot_ids = jnp.arange(expert_total * capacity, dtype=jnp.int32)
    picks = target[:, :, None] == slot_ids[None, None, :]
    dispatch = jnp.any(picks, axis=1).astype(jnp.bfloat16)
    outgoing = (
        lax.dot_general(
            dispatch, normed, (((0,), (0,)), ((), ())), preferred_element_type=jnp.float32
        )
        .astype(jnp.bfloat16)
        .reshape(expert_total, capacity, model_width)
    )
    arrived = lax.all_to_all(outgoing, "exp", split_axis=0, concat_axis=0, tiled=True)
    slot_count = arrived.shape[1]
    grouped = arrived.reshape(exp_size, local_experts, slot_count, model_width)
    gate_up = jnp.einsum("seid,edf->seif", grouped, w_gate_up, preferred_element_type=jnp.float32)
    acted = (jax.nn.silu(gate_up[..., :FF]) * gate_up[..., FF:]).astype(jnp.bfloat16)
    produced = jnp.einsum(
        "seif,efd->seid", acted, w_down, preferred_element_type=jnp.float32
    ).astype(jnp.bfloat16)
    returned = lax.all_to_all(
        produced.reshape(expert_total, slot_count, model_width),
        "exp",
        split_axis=0,
        concat_axis=0,
        tiled=True,
    )
    selected = jnp.einsum(
        "tks,sd->tkd",
        picks.astype(jnp.bfloat16),
        returned.reshape(expert_total * capacity, model_width),
        preferred_element_type=jnp.float32,
    )
    weighted = jnp.sum(gate_weights[:, :, None] * selected, axis=1)
    return (hidden_f + weighted).astype(jnp.bfloat16)


def solution(mesh):
    return jax.shard_map(
        body,
        mesh=mesh,
        in_specs=(
            P(("ctx", "exp"), None),
            P("ctx", "exp"),
            P("ctx", None),
            P("ctx", None),
            P("ctx", None),
            P("exp", None),
            P(),
            P("exp", None, None),
            P("exp", None, None),
            P(("ctx", "exp"), None),
            P(("ctx", "exp"), None),
        ),
        out_specs=P(("ctx", "exp"), None),
        check_vma=False,
    )
```

profile of v0, /device:TPU:24, one launch (start us, length us, event | category | flops | bytes accessed | tf_op | source)
XLA Modules:
  0.0 332.3 jit_solution(14435936207173884316)
XLA Ops:
  16.0 4.5 %bitcast_add_fusion.1 = f32[256,2,8,128]{0,3,2,1:T(8,128)} fusion(bf16[256,2,128,1]{0,2,3,1:T(8,128)(2,1)S(1)} %bitcast.136, f32[2,256,256,8]{2,1,3,0:T(8,128)} %copy-done, f32[256,2,8]{0,2,1:T(8,128)S(1)} %broadcast_maximum_fusion, pred[256,256]{0,1:T(8,128)(4,1)S(1)} %copy.62, f32[256,2,8]{0,2,1:T(8,128)S(1)} %get-tuple-element.344), kind=kOutput, calls=%fused_computation.44 | convolution fusion | flops 273154048 | bytes 6520832 | tf_op jit(solution)/shard_map/skgt,tkd->skgd/dot_general | solution.py:76
  22.4 196.6 %while.23 = (s32[]{:T(128)}, f32[256,2,8]{0,2,1:T(8,128)S(1)}, f32[256,2,8]{0,2,1:T(8,128)}, f32[256,2,8,128]{3,0,2,1:T(8,128)S(1)}, bf16[256,512]{0,1:T(8,128)(...) while((s32[]{:T(128)}, f32[256,2,8]{0,2,1:T(8,128)S(1)}, ...), condition=%wide.region_7.8_spmd.clone, body=%wide.region_3.7_spmd.clone.sunk | while | flops 549605120 | bytes 20979140 | solution.py:115
  22.4 1.9 collective-permute-start
  25.4 5.8 %collective-permute-done = bf16[256,512]{0,1:T(8,128)(2,1)S(1)} collective-permute-done((bf16[256,512]{0,1:T(8,128)(2,1)}, bf16[256,512]{0,1:T(8,128)(2,1)S(1)}, u32[]{:S(2)}, u32[]{:S(2)}) %collective-permute-start) | collective-permute-done | bytes 262176 | tf_op jit(solution)/shard_map/while/body/eval_jaxpr/ppermute | solution.py:21
  38.6 5.8 %collective-permute-done = bf16[256,512]{0,1:T(8,128)(2,1)S(1)} collective-permute-done((bf16[256,512]{0,1:T(8,128)(2,1)}, bf16[256,512]{0,1:T(8,128)(2,1)S(1)}, u32[]{:S(2)}, u32[]{:S(2)}) %collective-permute-start) | collective-permute-done | bytes 262176 | tf_op jit(solution)/shard_map/while/body/eval_jaxpr/ppermute | solution.py:21
  51.7 5.8 %collective-permute-done = bf16[256,512]{0,1:T(8,128)(2,1)S(1)} collective-permute-done((bf16[256,512]{0,1:T(8,128)(2,1)}, bf16[256,512]{0,1:T(8,128)(2,1)S(1)}, u32[]{:S(2)}, u32[]{:S(2)}) %collective-permute-start) | collective-permute-done | bytes 262176 | tf_op jit(solution)/shard_map/while/body/eval_jaxpr/ppermute | solution.py:21
  64.8 5.8 %collective-permute-done = bf16[256,512]{0,1:T(8,128)(2,1)S(1)} collective-permute-done((bf16[256,512]{0,1:T(8,128)(2,1)}, bf16[256,512]{0,1:T(8,128)(2,1)S(1)}, u32[]{:S(2)}, u32[]{:S(2)}) %collective-permute-start) | collective-permute-done | bytes 262176 | tf_op jit(solution)/shard_map/while/body/eval_jaxpr/ppermute | solution.py:21
  77.9 5.8 %collective-permute-done = bf16[256,512]{0,1:T(8,128)(2,1)S(1)} collective-permute-done((bf16[256,512]{0,1:T(8,128)(2,1)}, bf16[256,512]{0,1:T(8,128)(2,1)S(1)}, u32[]{:S(2)}, u32[]{:S(2)}) %collective-permute-start) | collective-permute-done | bytes 262176 | tf_op jit(solution)/shard_map/while/body/eval_jaxpr/ppermute | solution.py:21
  91.0 5.8 %collective-permute-done = bf16[256,512]{0,1:T(8,128)(2,1)S(1)} collective-permute-done((bf16[256,512]{0,1:T(8,128)(2,1)}, bf16[256,512]{0,1:T(8,128)(2,1)S(1)}, u32[]{:S(2)}, u32[]{:S(2)}) %collective-permute-start) | collective-permute-done | bytes 262176 | tf_op jit(solution)/shard_map/while/body/eval_jaxpr/ppermute | solution.py:21
  104.1 5.8 %collective-permute-done = bf16[256,512]{0,1:T(8,128)(2,1)S(1)} collective-permute-done((bf16[256,512]{0,1:T(8,128)(2,1)}, bf16[256,512]{0,1:T(8,128)(2,1)S(1)}, u32[]{:S(2)}, u32[]{:S(2)}) %collective-permute-start) | collective-permute-done | bytes 262176 | tf_op jit(solution)/shard_map/while/body/eval_jaxpr/ppermute | solution.py:21
  117.2 5.8 %collective-permute-done = bf16[256,512]{0,1:T(8,128)(2,1)S(1)} collective-permute-done((bf16[256,512]{0,1:T(8,128)(2,1)}, bf16[256,512]{0,1:T(8,128)(2,1)S(1)}, u32[]{:S(2)}, u32[]{:S(2)}) %collective-permute-start) | collective-permute-done | bytes 262176 | tf_op jit(solution)/shard_map/while/body/eval_jaxpr/ppermute | solution.py:21
  130.3 5.8 %collective-permute-done = bf16[256,512]{0,1:T(8,128)(2,1)S(1)} collective-permute-done((bf16[256,512]{0,1:T(8,128)(2,1)}, bf16[256,512]{0,1:T(8,128)(2,1)S(1)}, u32[]{:S(2)}, u32[]{:S(2)}) %collective-permute-start) | collective-permute-done | bytes 262176 | tf_op jit(solution)/shard_map/while/body/eval_jaxpr/ppermute | solution.py:21
  143.4 5.8 %collective-permute-done = bf16[256,512]{0,1:T(8,128)(2,1)S(1)} collective-permute-done((bf16[256,512]{0,1:T(8,128)(2,1)}, bf16[256,512]{0,1:T(8,128)(2,1)S(1)}, u32[]{:S(2)}, u32[]{:S(2)}) %collective-permute-start) | collective-permute-done | bytes 262176 | tf_op jit(solution)/shard_map/while/body/eval_jaxpr/ppermute | solution.py:21
  156.5 5.8 %collective-permute-done = bf16[256,512]{0,1:T(8,128)(2,1)S(1)} collective-permute-done((bf16[256,512]{0,1:T(8,128)(2,1)}, bf16[256,512]{0,1:T(8,128)(2,1)S(1)}, u32[]{:S(2)}, u32[]{:S(2)}) %collective-permute-start) | collective-permute-done | bytes 262176 | tf_op jit(solution)/shard_map/while/body/eval_jaxpr/ppermute | solution.py:21
  169.6 5.8 %collective-permute-done = bf16[256,512]{0,1:T(8,128)(2,1)S(1)} collective-permute-done((bf16[256,512]{0,1:T(8,128)(2,1)}, bf16[256,512]{0,1:T(8,128)(2,1)S(1)}, u32[]{:S(2)}, u32[]{:S(2)}) %collective-permute-start) | collective-permute-done | bytes 262176 | tf_op jit(solution)/shard_map/while/body/eval_jaxpr/ppermute | solution.py:21
  182.7 5.8 %collective-permute-done = bf16[256,512]{0,1:T(8,128)(2,1)S(1)} collective-permute-done((bf16[256,512]{0,1:T(8,128)(2,1)}, bf16[256,512]{0,1:T(8,128)(2,1)S(1)}, u32[]{:S(2)}, u32[]{:S(2)}) %collective-permute-start) | collective-permute-done | bytes 262176 | tf_op jit(solution)/shard_map/while/body/eval_jaxpr/ppermute | solution.py:21
  195.8 5.8 %collective-permute-done = bf16[256,512]{0,1:T(8,128)(2,1)S(1)} collective-permute-done((bf16[256,512]{0,1:T(8,128)(2,1)}, bf16[256,512]{0,1:T(8,128)(2,1)S(1)}, u32[]{:S(2)}, u32[]{:S(2)}) %collective-permute-start) | collective-permute-done | bytes 262176 | tf_op jit(solution)/shard_map/while/body/eval_jaxpr/ppermute | solution.py:21
  208.9 5.8 %collective-permute-done = bf16[256,512]{0,1:T(8,128)(2,1)S(1)} collective-permute-done((bf16[256,512]{0,1:T(8,128)(2,1)}, bf16[256,512]{0,1:T(8,128)(2,1)S(1)}, u32[]{:S(2)}, u32[]{:S(2)}) %collective-permute-start) | collective-permute-done | bytes 262176 | tf_op jit(solution)/shard_map/while/body/eval_jaxpr/ppermute | solution.py:21
  222.7 6.8 %convolution_convert_fusion.1 = bf16[256,2048]{1,0:T(8,128)(2,1)} fusion(bf16[256,2048]{0,1:T(8,128)(2,1)S(1)} %bitcast.133, bf16[2048,2048]{1,0:T(8,128)(2,1)} %param.18), kind=kOutput, calls=%fused_computation.42 | convolution fusion | flops 2148007936 | bytes 10485760 | tf_op jit(solution)/shard_map/dot_general | solution.py:124
  231.3 18.8 %reduce-scatter.2.cloned.1.call-done = bf16[128,2048]{1,0:T(8,128)(2,1)} async-done(((bf16[256,2048]{1,0:T(8,128)(2,1)}), bf16[128,2048]{1,0:T(8,128)(2,1)}) %reduce-scatter.2.cloned.1.call-update) | async-done | bytes 524304 | tf_op jit(solution)/shard_map/reduce_scatter | solution.py:123
  252.3 27.7 %all_to_all.10 = bf16[8,64,2048]{2,1,0:T(8,128)(2,1)S(1)} all-to-all(bf16[8,64,2048]{2,1,0:T(8,128)(2,1)S(1)} %bitcast.131), channel_id=1, replica_groups=mesh['ctx'=16,'exp'=2] {'exp'}, dimensions={0} | all-to-all | bytes 4194304 | tf_op jit(solution)/shard_map/all_to_all | solution.py:155
  279.9 10.0 %fusion.24 = f32[2,4,64,1536]{3,2,0,1:T(8,128)S(1)} fusion(bf16[4,2048,1536]{2,1,0:T(8,128)(2,1)} %param.20, bf16[2,4,64,2048]{3,2,1,0:T(8,128)(2,1)S(1)} %bitcast.126), kind=kOutput, calls=%fused_computation.35 | convolution fusion | flops 3221225472 | bytes 30408704 | tf_op jit(solution)/shard_map/seid,edf->seif/dot_general | solution.py:158
  289.9 6.7 %fusion.32 = bf16[2,4,64,2048]{3,2,0,1:T(8,128)(2,1)S(1)} fusion(bf16[4,768,2048]{2,1,0:T(8,128)(2,1)} %param.21, f32[2,4,64,1536]{3,2,0,1:T(8,128)S(1)} %fusion.24), kind=kOutput, calls=%fused_computation.40 | convolution fusion | flops 1614020608 | bytes 17825792 | tf_op jit(solution)/shard_map/seif,efd->seid/dot_general | solution.py:160
  296.8 26.8 %all_to_all.11 = bf16[8,64,2048]{2,1,0:T(8,128)(2,1)S(1)} all-to-all(bf16[8,64,2048]{2,1,0:T(8,128)(2,1)S(1)} %bitcast.132), channel_id=1, replica_groups=mesh['ctx'=16,'exp'=2] {'exp'}, dimensions={0} | all-to-all | bytes 4194304 | tf_op jit(solution)/shard_map/all_to_all | solution.py:163
  (320 shorter events, 126.9 us)
Async XLA Ops:
  6.5 243.5 %reduce-scatter.2.cloned.1.call-start = ((), (), s32[]{:S(2)}) async-start(), calls=%async_computation.3 | async-start | bytes 1572864 | tf_op jit(solution)/shard_map/reduce_scatter | solution.py:123
  11.7 1.9 copy-start
  22.4 8.8 %collective-permute-start = (bf16[256,512]{0,1:T(8,128)(2,1)}, bf16[256,512]{0,1:T(8,128)(2,1)S(1)}, u32[]{:S(2)}, u32[]{:S(2)}) collective-permute-start(bf16[256,512]{0,1:T(8,128)(2,1)} %get-tuple-element.442), channel_id=1, source_target_pairs={{0,2},{2,4},{4,6},{6,8},{8,10},{10,12},{12,14},{14,16},{16,18},{18... | collective-permute-start | bytes 786440 | tf_op jit(solution)/shard_map/while/body/eval_jaxpr/ppermute | solution.py:21
  33.0 1.8 copy-start.2
  35.5 8.8 %collective-permute-start = (bf16[256,512]{0,1:T(8,128)(2,1)}, bf16[256,512]{0,1:T(8,128)(2,1)S(1)}, u32[]{:S(2)}, u32[]{:S(2)}) collective-permute-start(bf16[256,512]{0,1:T(8,128)(2,1)} %get-tuple-element.442), channel_id=1, source_target_pairs={{0,2},{2,4},{4,6},{6,8},{8,10},{10,12},{12,14},{14,16},{16,18},{18... | collective-permute-start | bytes 786440 | tf_op jit(solution)/shard_map/while/body/eval_jaxpr/ppermute | solution.py:21
  48.6 8.8 %collective-permute-start = (bf16[256,512]{0,1:T(8,128)(2,1)}, bf16[256,512]{0,1:T(8,128)(2,1)S(1)}, u32[]{:S(2)}, u32[]{:S(2)}) collective-permute-start(bf16[256,512]{0,1:T(8,128)(2,1)} %get-tuple-element.442), channel_id=1, source_target_pairs={{0,2},{2,4},{4,6},{6,8},{8,10},{10,12},{12,14},{14,16},{16,18},{18... | collective-permute-start | bytes 786440 | tf_op jit(solution)/shard_map/while/body/eval_jaxpr/ppermute | solution.py:21
  61.7 8.8 %collective-permute-start = (bf16[256,512]{0,1:T(8,128)(2,1)}, bf16[256,512]{0,1:T(8,128)(2,1)S(1)}, u32[]{:S(2)}, u32[]{:S(2)}) collective-permute-start(bf16[256,512]{0,1:T(8,128)(2,1)} %get-tuple-element.442), channel_id=1, source_target_pairs={{0,2},{2,4},{4,6},{6,8},{8,10},{10,12},{12,14},{14,16},{16,18},{18... | collective-permute-start | bytes 786440 | tf_op jit(solution)/shard_map/while/body/eval_jaxpr/ppermute | solution.py:21
  74.8 8.8 %collective-permute-start = (bf16[256,512]{0,1:T(8,128)(2,1)}, bf16[256,512]{0,1:T(8,128)(2,1)S(1)}, u32[]{:S(2)}, u32[]{:S(2)}) collective-permute-start(bf16[256,512]{0,1:T(8,128)(2,1)} %get-tuple-element.442), channel_id=1, source_target_pairs={{0,2},{2,4},{4,6},{6,8},{8,10},{10,12},{12,14},{14,16},{16,18},{18... | collective-permute-start | bytes 786440 | tf_op jit(solution)/shard_map/while/body/eval_jaxpr/ppermute | solution.py:21
  88.0 8.8 %collective-permute-start = (bf16[256,512]{0,1:T(8,128)(2,1)}, bf16[256,512]{0,1:T(8,128)(2,1)S(1)}, u32[]{:S(2)}, u32[]{:S(2)}) collective-permute-start(bf16[256,512]{0,1:T(8,128)(2,1)} %get-tuple-element.442), channel_id=1, source_target_pairs={{0,2},{2,4},{4,6},{6,8},{8,10},{10,12},{12,14},{14,16},{16,18},{18... | collective-permute-start | bytes 786440 | tf_op jit(solution)/shard_map/while/body/eval_jaxpr/ppermute | solution.py:21
  101.1 8.8 %collective-permute-start = (bf16[256,512]{0,1:T(8,128)(2,1)}, bf16[256,512]{0,1:T(8,128)(2,1)S(1)}, u32[]{:S(2)}, u32[]{:S(2)}) collective-permute-start(bf16[256,512]{0,1:T(8,128)(2,1)} %get-tuple-element.442), channel_id=1, source_target_pairs={{0,2},{2,4},{4,6},{6,8},{8,10},{10,12},{12,14},{14,16},{16,18},{18... | collective-permute-start | bytes 786440 | tf_op jit(solution)/shard_map/while/body/eval_jaxpr/ppermute | solution.py:21
  114.2 8.8 %collective-permute-start = (bf16[256,512]{0,1:T(8,128)(2,1)}, bf16[256,512]{0,1:T(8,128)(2,1)S(1)}, u32[]{:S(2)}, u32[]{:S(2)}) collective-permute-start(bf16[256,512]{0,1:T(8,128)(2,1)} %get-tuple-element.442), channel_id=1, source_target_pairs={{0,2},{2,4},{4,6},{6,8},{8,10},{10,12},{12,14},{14,16},{16,18},{18... | collective-permute-start | bytes 786440 | tf_op jit(solution)/shard_map/while/body/eval_jaxpr/ppermute | solution.py:21
  124.8 1.8 copy-start.2
  127.3 8.8 %collective-permute-start = (bf16[256,512]{0,1:T(8,128)(2,1)}, bf16[256,512]{0,1:T(8,128)(2,1)S(1)}, u32[]{:S(2)}, u32[]{:S(2)}) collective-permute-start(bf16[256,512]{0,1:T(8,128)(2,1)} %get-tuple-element.442), channel_id=1, source_target_pairs={{0,2},{2,4},{4,6},{6,8},{8,10},{10,12},{12,14},{14,16},{16,18},{18... | collective-permute-start | bytes 786440 | tf_op jit(solution)/shard_map/while/body/eval_jaxpr/ppermute | solution.py:21
  140.4 8.8 %collective-permute-start = (bf16[256,512]{0,1:T(8,128)(2,1)}, bf16[256,512]{0,1:T(8,128)(2,1)S(1)}, u32[]{:S(2)}, u32[]{:S(2)}) collective-permute-start(bf16[256,512]{0,1:T(8,128)(2,1)} %get-tuple-element.442), channel_id=1, source_target_pairs={{0,2},{2,4},{4,6},{6,8},{8,10},{10,12},{12,14},{14,16},{16,18},{18... | collective-permute-start | bytes 786440 | tf_op jit(solution)/shard_map/while/body/eval_jaxpr/ppermute | solution.py:21
  153.5 8.8 %collective-permute-start = (bf16[256,512]{0,1:T(8,128)(2,1)}, bf16[256,512]{0,1:T(8,128)(2,1)S(1)}, u32[]{:S(2)}, u32[]{:S(2)}) collective-permute-start(bf16[256,512]{0,1:T(8,128)(2,1)} %get-tuple-element.442), channel_id=1, source_target_pairs={{0,2},{2,4},{4,6},{6,8},{8,10},{10,12},{12,14},{14,16},{16,18},{18... | collective-permute-start | bytes 786440 | tf_op jit(solution)/shard_map/while/body/eval_jaxpr/ppermute | solution.py:21
  166.6 8.8 %collective-permute-start = (bf16[256,512]{0,1:T(8,128)(2,1)}, bf16[256,512]{0,1:T(8,128)(2,1)S(1)}, u32[]{:S(2)}, u32[]{:S(2)}) collective-permute-start(bf16[256,512]{0,1:T(8,128)(2,1)} %get-tuple-element.442), channel_id=1, source_target_pairs={{0,2},{2,4},{4,6},{6,8},{8,10},{10,12},{12,14},{14,16},{16,18},{18... | collective-permute-start | bytes 786440 | tf_op jit(solution)/shard_map/while/body/eval_jaxpr/ppermute | solution.py:21
  179.7 8.8 %collective-permute-start = (bf16[256,512]{0,1:T(8,128)(2,1)}, bf16[256,512]{0,1:T(8,128)(2,1)S(1)}, u32[]{:S(2)}, u32[]{:S(2)}) collective-permute-start(bf16[256,512]{0,1:T(8,128)(2,1)} %get-tuple-element.442), channel_id=1, source_target_pairs={{0,2},{2,4},{4,6},{6,8},{8,10},{10,12},{12,14},{14,16},{16,18},{18... | collective-permute-start | bytes 786440 | tf_op jit(solution)/shard_map/while/body/eval_jaxpr/ppermute | solution.py:21
  192.8 8.8 %collective-permute-start = (bf16[256,512]{0,1:T(8,128)(2,1)}, bf16[256,512]{0,1:T(8,128)(2,1)S(1)}, u32[]{:S(2)}, u32[]{:S(2)}) collective-permute-start(bf16[256,512]{0,1:T(8,128)(2,1)} %get-tuple-element.442), channel_id=1, source_target_pairs={{0,2},{2,4},{4,6},{6,8},{8,10},{10,12},{12,14},{14,16},{16,18},{18... | collective-permute-start | bytes 786440 | tf_op jit(solution)/shard_map/while/body/eval_jaxpr/ppermute | solution.py:21
  205.9 8.8 %collective-permute-start = (bf16[256,512]{0,1:T(8,128)(2,1)}, bf16[256,512]{0,1:T(8,128)(2,1)S(1)}, u32[]{:S(2)}, u32[]{:S(2)}) collective-permute-start(bf16[256,512]{0,1:T(8,128)(2,1)} %get-tuple-element.442), channel_id=1, source_target_pairs={{0,2},{2,4},{4,6},{6,8},{8,10},{10,12},{12,14},{14,16},{16,18},{18... | collective-permute-start | bytes 786440 | tf_op jit(solution)/shard_map/while/body/eval_jaxpr/ppermute | solution.py:21
  219.0 1.9 copy-start.3
  222.7 6.9 %copy-start.6 = (s32[128,2]{0,1:T(2,128)S(1)}, s32[128,2]{0,1:T(2,128)}, u32[]{:S(2)}) copy-start(s32[128,2]{0,1:T(2,128)} %param.22) | copy-start | bytes 3076
  222.7 27.4 %copy-start.4 = (bf16[128,2048]{1,0:T(8,128)(2,1)S(1)}, bf16[128,2048]{1,0:T(8,128)(2,1)}, u32[]{:S(2)}) copy-start(bf16[128,2048]{1,0:T(8,128)(2,1)} %param.13) | copy-start | bytes 1572868
  222.7 28.7 %copy-start.5 = (f32[2048]{0:T(1024)S(1)}, f32[2048]{0:T(1024)}, u32[]{:S(2)}) copy-start(f32[2048]{0:T(1024)} %param.19) | copy-start | bytes 24580
  296.7 26.9 %copy-start.7 = (f32[128,2]{0,1:T(2,128)S(1)}, f32[128,2]{0,1:T(2,128)}, u32[]{:S(2)}) copy-start(f32[128,2]{0,1:T(2,128)} %param.23) | copy-start | bytes 3076
  (28 other events, 49.8 us)
Sparse Core Ops, SparseCore 0:
  229.7 20.3 reduce-scatter.1
where the time goes:
time: 335 us; the launch traced here: 332 us
  waiting for transfers between devices  105 us (31%)
  matrix products  69.8 us (21%)
  blocking collectives  54.4 us (16%)
  other arithmetic  34.8 us (10%)
  starting transfers between devices  28.6 us (9%)
  local copies, waits for them, and re-layouts  23.7 us (7%)
  between operations  13.6 us (4%)
    ppermute x15, waiting for transfers between devices, shifted(): lax.ppermute(value, axis, [(source, source + steps) for source in range(f...  86.5 us
    dot_general x16, matrix products, update(): jnp.einsum('skgt,tkd->skgd', weights.astype(jnp.bfloat16), value_part.res...  30.7 us
    ppermute x15, starting transfers between devices, shifted(): lax.ppermute(value, axis, [(source, source + steps) for source in range(f...  28.6 us
    all_to_all x1, blocking collectives, body(): lax.all_to_all(outgoing, 'exp', split_axis=0, concat_axis=0, tiled=True)  27.7 us
    all_to_all x1, blocking collectives, body(): lax.all_to_all(produced.reshape(expert_total, slot_count, model_width), '...  26.8 us
    reduce_scatter x1, waiting for transfers between devices, body(): lax.psum_scatter(jnp.dot(attended, out_weight, preferred_element_type=jnp...  18.8 us
    reduce_sum x16, other arithmetic, update(): weight_sum = weight_sum * shrink + jnp.sum(weights, axis=-1)  13.9 us
    dot_general x16, matrix products, update(): jnp.einsum('skgd,tkd->skgt', query_heads, key_part.reshape(row_count, kv_...  13.9 us
  transfers between devices with their start and end apart: 16, of which 16 were waited for; matrix products, arithmetic and copies ran while one was open for 5% of the time, Pallas kernels for 0%

commit v1 on v0

--- a/solution.py
+++ b/solution.py
@@ -3,6 +3,8 @@
 import jax
 import jax.numpy as jnp
 from jax import lax
+from jax.experimental import pallas as pl
+from jax.experimental.pallas import tpu as pltpu
 from jax.sharding import PartitionSpec as P
 
 HQ = 32
@@ -137,10 +139,10 @@
     model_width = normed.shape[1]
     route_count = expert_ids.shape[1]
     flat_ids = expert_ids.reshape(token_count * route_count)
-    onehot = (flat_ids[:, None] == jnp.arange(expert_total, dtype=jnp.int32)[None, :]).astype(
-        jnp.int32
-    )
-    slot_rank = jnp.sum((jnp.cumsum(onehot, axis=0) - onehot) * onehot, axis=1)
+    flat_count = flat_ids.shape[0]
+    order = jnp.arange(flat_count, dtype=jnp.int32)
+    ahead = (flat_ids[:, None] == flat_ids[None, :]) & (order[None, :] < order[:, None])
+    slot_rank = jnp.sum(ahead.astype(jnp.int32), axis=1)
     target = (flat_ids * capacity + slot_rank).reshape(token_count, route_count)
     slot_ids = jnp.arange(expert_total * capacity, dtype=jnp.int32)
     picks = target[:, :, None] == slot_ids[None, None, :]
@@ -177,9 +179,368 @@
     return (hidden_f + weighted).astype(jnp.bfloat16)
 
 
+MESH = pl.DeviceIdType.MESH
+TOK = 128
+ROWS = 256
+GROUP = HQ // KVH
+LOG2E = 1.4426950408889634
+COLS = 512
+ORDER = ((0, 0), (0, 1), (1, 0), (0, 2), (1, 1), (0, 3), (1, 2), (1, 3))
+
+
+def layer_kernel(
+    hid_ref, q_ref, k_ref, v_ref, blk_ref, list_ref, wo_ref, gain_ref, wgu_ref, wd_ref, ids_ref, gw_ref,
+    out_ref,
+    kv0, kv1, kcat, bias_s, q_s, att, wbuf, wgu_s, part_s, part_r, hid_s, nrm, act, ret_s, ret_r, g_s,
+    loc_sem, own_sem, w_sem, zs, xs, cs, kv_recv, hs, hr, gs, gr, ps, pr, rs, rr,
+):
+    c = lax.axis_index("ctx")
+    e = lax.axis_index("exp")
+    z = c // 4
+    x = (c // 2) % 2
+    core = c % 2
+    sibling = c + 1 - 2 * core
+    x_peer = c + 2 - 4 * x
+    kvs = (kv0, kv1)
+    width = wo_ref.shape[1]
+    chunks = width // COLS
+
+    def kv_rows(block):
+        return pl.ds(block * 2, 2)
+
+    own_rows = kv_rows(c)
+    mine = pl.ds(pl.multiple_of(e * TOK, TOK), TOK)
+    other = pl.ds(pl.multiple_of((1 - e) * TOK, TOK), TOK)
+
+    own = []
+    for h in range(2):
+        cols = pl.ds(pl.multiple_of(e * 2 * HD + h * HD, HD), HD)
+        own.append(pltpu.make_async_copy(k_ref.at[:, :, cols], kvs[h].at[own_rows, :, pl.ds(0, HD)], own_sem.at[2 * h]))
+        own.append(pltpu.make_async_copy(v_ref.at[:, :, cols], kvs[h].at[own_rows, :, pl.ds(HD, HD)], own_sem.at[2 * h + 1]))
+    for copy in own:
+        copy.start()
+    q_copy = pltpu.make_async_copy(q_ref, q_s, loc_sem.at[0])
+    hid_copy = pltpu.make_async_copy(hid_ref, hid_s.at[mine, :], loc_sem.at[1])
+    wo_copy = pltpu.make_async_copy(wo_ref, wbuf.at[pl.ds(0, wo_ref.shape[0]), :], loc_sem.at[2])
+    wd_copy = pltpu.make_async_copy(wd_ref, wbuf, loc_sem.at[3])
+    wgu_copies = [pltpu.make_async_copy(wgu_ref.at[i], wgu_s.at[i], w_sem.at[i]) for i in range(4)]
+
+    barrier = pltpu.get_barrier_semaphore()
+    pl.semaphore_signal(barrier, inc=1, device_id=(sibling, e), device_id_type=MESH)
+    pl.semaphore_signal(barrier, inc=1, device_id=(x_peer, e), device_id_type=MESH)
+    pl.semaphore_signal(barrier, inc=1, device_id=(c, 1 - e), device_id_type=MESH)
+
+    @pl.when(z > 0)
+    def _():
+        pl.semaphore_signal(barrier, inc=1, device_id=(c - 4, e), device_id_type=MESH)
+
+    @pl.when(z < 3)
+    def _():
+        pl.semaphore_signal(barrier, inc=1, device_id=(c + 4, e), device_id_type=MESH)
+
+    lane = lax.broadcasted_iota(jnp.int32, (TOK, HD), 1)
+    g_s[mine, :] = jnp.where(lane == ids_ref[:, 0:1], gw_ref[:, 0:1], 0.0) + jnp.where(
+        lane == ids_ref[:, 1:2], gw_ref[:, 1:2], 0.0
+    )
+    inner = (z > 0) & (z < 3)
+
+    @pl.when(inner)
+    def _():
+        pl.semaphore_wait(barrier, 5)
+
+    @pl.when(jnp.logical_not(inner))
+    def _():
+        pl.semaphore_wait(barrier, 4)
+
+    def send(h, block, send_sem, device):
+        rows = kv_rows(block)
+        return pltpu.make_async_remote_copy(
+            src_ref=kvs[h].at[rows], dst_ref=kvs[h].at[rows], send_sem=send_sem,
+            recv_sem=kv_recv.at[h, block], device_id=(device, e), device_id_type=MESH,
+        )
+
+    def line(k):
+        return (z - k) * 4 + x * 2 + core
+
+    def across(k):
+        return (z - k) * 4 + (1 - x) * 2 + core
+
+    def z_send(h, k):
+        return send(h, line(k), zs.at[h, k], c + 4)
+
+    def x_send(h, k):
+        return send(h, line(k), xs.at[h, k], x_peer)
+
+    def c_send(h, k):
+        return send(h, line(k), cs.at[h, k], sibling)
+
+    def c_send_across(h, k):
+        return send(h, across(k), cs.at[h, 4 + k], sibling)
+
+    hid_send = pltpu.make_async_remote_copy(
+        src_ref=hid_ref, dst_ref=hid_s.at[mine, :], send_sem=hs, recv_sem=hr,
+        device_id=(c, 1 - e), device_id_type=MESH,
+    )
+    g_send = pltpu.make_async_remote_copy(
+        src_ref=g_s.at[mine, :], dst_ref=g_s.at[mine, :], send_sem=gs, recv_sem=gr,
+        device_id=(c, 1 - e), device_id_type=MESH,
+    )
+
+    def relay(h, k):
+        @pl.when(z >= k)
+        def _():
+            if k > 0:
+                send(h, line(k), zs.at[h, k], sibling).wait_recv()
+
+            @pl.when(z < 3)
+            def _():
+                z_send(h, k).start()
+
+            x_send(h, k).start()
+            c_send(h, k).start()
+
+    def relay_across(h, k):
+        @pl.when(z >= k)
+        def _():
+            send(h, across(k), zs.at[h, k], sibling).wait_recv()
+            c_send_across(h, k).start()
+
+    for place, (h, k) in enumerate(ORDER):
+        if k == 0:
+            own[2 * h].wait()
+            own[2 * h + 1].wait()
+        relay(h, k)
+        if place == 0:
+            hid_send.start()
+            g_send.start()
+            q_copy.start()
+            hid_copy.start()
+            wo_copy.start()
+            for copy in wgu_copies:
+                copy.start()
+        if place > 0:
+            relay_across(*ORDER[place - 1])
+    relay_across(*ORDER[-1])
+    for h in range(2):
+        for k in range(4):
+            @pl.when(z >= k)
+            def _(h=h, k=k):
+                for xx in range(2):
+                    send(h, (z - k) * 4 + xx * 2 + 1 - core, zs.at[h, k], sibling).wait_recv()
+    q_copy.wait()
+
+    scale = LOG2E / math.sqrt(HD)
+    key_row = lax.broadcasted_iota(jnp.int32, (2 * BLK, BLK), 1)
+    query_row = lax.broadcasted_iota(jnp.int32, (2 * BLK, BLK), 0) % BLK
+    triangle = jnp.where(key_row <= query_row, 0.0, NEG_FILL).astype(jnp.float32)
+    picks = blk_ref.shape[1]
+    for t in range(2):
+        for j in range(1, picks):
+            listed = jnp.broadcast_to(list_ref[t : t + 1, j : j + 1], (1, BLK))
+            again = jnp.zeros((1, BLK), jnp.float32)
+            for i in range(j):
+                again += jnp.where(listed == list_ref[t : t + 1, i : i + 1], 1.0, 0.0)
+            bias_s[t, :, (j - 1) * BLK : j * BLK] = jnp.where(again > 0.0, NEG_FILL, 0.0)
+
+    @pl.loop(0, 2)
+    def _(t):
+        rows = pl.ds(pl.multiple_of(t * BLK, BLK), BLK)
+        listed = [blk_ref[t, j] for j in range(picks)]
+        bias = bias_s[t]
+        for h in range(2):
+            for j in range(picks):
+                kcat[j * BLK : (j + 1) * BLK, :] = kvs[h][listed[j]]
+
+            @pl.loop(0, GROUP // 4)
+            def _(quad):
+                for half in range(2):
+                    first = pl.multiple_of((h * GROUP + quad * 4 + half * 2) * HD, HD)
+                    second = pl.multiple_of((h * GROUP + quad * 4 + half * 2 + 1) * HD, HD)
+                    queries = jnp.concatenate([q_s[rows, pl.ds(first, HD)], q_s[rows, pl.ds(second, HD)]], axis=0)
+                    scores = lax.dot_general(
+                        queries, kcat[:, :HD], (((1,), (1,)), ((), ())), preferred_element_type=jnp.float32
+                    )
+                    near = scores[:, :BLK] * scale + triangle
+                    far = scores[:, BLK:] * scale + bias
+                    top = jnp.maximum(
+                        jnp.max(near, axis=1, keepdims=True), jnp.max(far, axis=1, keepdims=True)
+                    )
+                    near = jnp.exp2(near - top)
+                    far = jnp.exp2(far - top)
+                    total = jnp.sum(near, axis=1, keepdims=True) + jnp.sum(far, axis=1, keepdims=True)
+                    weights = jnp.concatenate([near.astype(jnp.bfloat16), far.astype(jnp.bfloat16)], axis=1)
+                    mixed = jnp.dot(weights, kcat[:, HD:], preferred_element_type=jnp.float32) / total
+                    mixed = mixed.astype(jnp.bfloat16)
+                    att[rows, pl.ds(first, HD)] = mixed[:BLK]
+                    att[rows, pl.ds(second, HD)] = mixed[BLK:]
+
+    def chunk(n):
+        return pl.ds(pl.multiple_of(n * COLS, COLS), COLS)
+
+    def part_send(which, n):
+        rows = mine if which == 0 else other
+        return pltpu.make_async_remote_copy(
+            src_ref=part_s.at[rows, chunk(n)], dst_ref=part_r.at[rows, chunk(n)], send_sem=ps.at[which, n],
+            recv_sem=pr.at[which, n], device_id=(c, 1 - e), device_id_type=MESH,
+        )
+
+    def part_recv(which, n):
+        rows = other if which == 0 else mine
+        return pltpu.make_async_remote_copy(
+            src_ref=part_s.at[rows, chunk(n)], dst_ref=part_r.at[rows, chunk(n)], send_sem=ps.at[which, n],
+            recv_sem=pr.at[which, n], device_id=(c, 1 - e), device_id_type=MESH,
+        )
+
+    def ret_send(n):
+        return pltpu.make_async_remote_copy(
+            src_ref=ret_s.at[:, chunk(n)], dst_ref=ret_r.at[:, chunk(n)], send_sem=rs.at[n],
+            recv_sem=rr.at[n], device_id=(c, 1 - e), device_id_type=MESH,
+        )
+
+    wo_copy.wait()
+    depth = wo_ref.shape[0]
+
+    @pl.loop(0, chunks)
+    def _(n):
+        product = jnp.dot(att[...], wbuf[:depth, chunk(n)], preferred_element_type=jnp.float32)
+        part_s[:, chunk(n)] = product.astype(jnp.bfloat16)
+        part_send(0, n).start()
+
+    @pl.loop(0, chunks)
+    def _(n):
+        part_send(1, n).start()
+
+    wd_copy.start()
+    hid_copy.wait()
+    hid_send.wait()
+    g_send.wait()
+    for copy in wgu_copies:
+        copy.wait()
+
+    for turn in range(2):
+        rows = other if turn == 0 else mine
+
+        @pl.loop(0, chunks)
+        def _(n, turn=turn):
+            part_recv(turn, n).wait_recv()
+
+        hidden = (
+            hid_s[rows, :].astype(jnp.float32)
+            + (part_s[rows, :].astype(jnp.float32) + part_r[rows, :].astype(jnp.float32))
+        ).astype(jnp.bfloat16)
+        hid_s[rows, :] = hidden
+        hidden_f = hidden.astype(jnp.float32)
+        mean_square = jnp.mean(hidden_f * hidden_f, axis=1, keepdims=True)
+        nrm[...] = (hidden_f * lax.rsqrt(mean_square + 1e-06) * gain_ref[...]).astype(jnp.bfloat16)
+
+        @pl.loop(0, 4)
+        def _(i):
+            for n in range(FF // 256):
+                gate = jnp.dot(
+                    nrm[...], wgu_s[i, :, n * 256 : (n + 1) * 256], preferred_element_type=jnp.float32
+                )
+                up = jnp.dot(
+                    nrm[...], wgu_s[i, :, FF + n * 256 : FF + (n + 1) * 256], preferred_element_type=jnp.float32
+                )
+                acted = gate / (1.0 + jnp.exp(-gate)) * up
+                act[:, pl.ds(pl.multiple_of(i * FF + n * 256, 256), 256)] = acted.astype(jnp.bfloat16)
+
+        if turn == 0:
+            wd_copy.wait()
+        gates = g_s[rows, :]
+        shares = [
+            jnp.sum(jnp.where(lane == e * 4 + i, gates, 0.0), axis=1, keepdims=True) for i in range(4)
+        ]
+
+        @pl.loop(0, chunks)
+        def _(n, turn=turn, rows=rows, shares=shares):
+            total = jnp.zeros((TOK, COLS), jnp.float32)
+            for i in range(4):
+                total += shares[i] * jnp.dot(
+                    act[:, i * FF : (i + 1) * FF], wbuf[i * FF : (i + 1) * FF, chunk(n)],
+                    preferred_element_type=jnp.float32,
+                )
+            if turn == 0:
+                ret_s[:, chunk(n)] = total.astype(jnp.bfloat16)
+                ret_send(n).start()
+            else:
+                ret_send(n).wait_recv()
+                total += ret_r[:, chunk(n)].astype(jnp.float32)
+                out_ref[:, chunk(n)] = (hid_s[rows, chunk(n)].astype(jnp.float32) + total).astype(jnp.bfloat16)
+
+    @pl.loop(0, chunks)
+    def _(n):
+        part_send(0, n).wait_send()
+        part_send(1, n).wait_send()
+        ret_send(n).wait_send()
+
+    for h in range(2):
+        for k in range(4):
+            @pl.when(z >= k)
+            def _(h=h, k=k):
+                @pl.when(z < 3)
+                def _():
+                    z_send(h, k).wait_send()
+
+                x_send(h, k).wait_send()
+                c_send(h, k).wait_send()
+                c_send_across(h, k).wait_send()
+
+
+def fused_body(
+    hidden_in, queries, keys, values, blocks, out_weight, norm_gain, w_gate_up, w_down, expert_ids, gate_weights
+):
+    tokens, width = hidden_in.shape
+    experts = w_gate_up.shape[0]
+    seq = keys.shape[0] * lax.axis_size("ctx")
+    bf16 = jnp.bfloat16
+    dma = pltpu.SemaphoreType.DMA
+    chunks = width // COLS
+    hbm = pl.BlockSpec(memory_space=pl.ANY)
+    vmem = pl.BlockSpec(memory_space=pltpu.VMEM)
+    smem = pl.BlockSpec(memory_space=pltpu.SMEM)
+    return pl.pallas_call(
+        layer_kernel,
+        out_shape=jax.ShapeDtypeStruct((tokens, width), bf16),
+        in_specs=[hbm, hbm, hbm, hbm, smem, vmem, hbm, vmem, hbm, hbm, vmem, vmem],
+        out_specs=vmem,
+        scratch_shapes=[
+            pltpu.VMEM((seq // BLK, BLK, 2 * HD), bf16),
+            pltpu.VMEM((seq // BLK, BLK, 2 * HD), bf16),
+            pltpu.VMEM((blocks.shape[1] * BLK, 2 * HD), bf16),
+            pltpu.VMEM((2, 1, (blocks.shape[1] - 1) * BLK), jnp.float32),
+            pltpu.VMEM(queries.shape, bf16),
+            pltpu.VMEM(queries.shape, bf16),
+            pltpu.VMEM((experts * FF, width), bf16),
+            pltpu.VMEM(w_gate_up.shape, bf16),
+            pltpu.VMEM((2 * tokens, width), bf16),
+            pltpu.VMEM((2 * tokens, width), bf16),
+            pltpu.VMEM((2 * tokens, width), bf16),
+            pltpu.VMEM((tokens, width), bf16),
+            pltpu.VMEM((tokens, experts * FF), bf16),
+            pltpu.VMEM((tokens, width), bf16),
+            pltpu.VMEM((tokens, width), bf16),
+            pltpu.VMEM((2 * tokens, HD), jnp.float32),
+            dma((4,)), dma((4,)), dma((4,)),
+            dma((2, 4)), dma((2, 4)), dma((2, 8)), dma((2, 16)),
+            dma, dma, dma, dma,
+            dma((2, chunks)), dma((2, chunks)), dma((chunks,)), dma((chunks,)),
+        ],
+        compiler_params=pltpu.CompilerParams(
+            collective_id=0, has_side_effects=True, vmem_limit_bytes=60 * 2**20
+        ),
+        cost_estimate=pl.CostEstimate(flops=14 * 10**9, bytes_accessed=5 * 10**7, transcendentals=5 * 10**6),
+    )(
+        hidden_in, queries, keys.reshape(2, BLK, -1), values.reshape(2, BLK, -1), blocks, blocks, out_weight,
+        norm_gain.reshape(1, width),
+        w_gate_up, w_down.reshape(experts * FF, width), expert_ids, gate_weights,
+    )
+
+
 def solution(mesh):
+    fits = mesh.shape["ctx"] == 16 and mesh.shape["exp"] == 2
     return jax.shard_map(
-        body,
+        fused_body if fits else body,
         mesh=mesh,
         in_specs=(
             P(("ctx", "exp"), None),

time: 335 us -> 80.6 us (0.24)
  waiting for transfers between devices: 105 us -> 0 us
  Pallas kernels: 0 us -> 75.1 us
  matrix products: 69.8 us -> 0 us
  blocking collectives: 54.4 us -> 0 us
  other arithmetic: 34.8 us -> 0 us
  starting transfers between devices: 28.6 us -> 0 us
  local copies, waits for them, and re-layouts: 23.7 us -> 4.7 us
  between operations: 13.6 us -> 0.01 us
    ppermute x15 -> x0, waiting for transfers between devices: 86.5 us -> none  [shifted(): lax.ppermute(value, axis, [(source, source + steps) for source in range(f...]
    pallas_call x0 -> x1, Pallas kernels: none -> 75.1 us  [fused_body(): pl.pallas_call(layer_kernel, out_shape=jax.ShapeDtypeStruct((tokens, widt...]
    dot_general x37 -> x0, matrix products: 69.8 us -> none  [the longest x16 30.7 us: update(): jnp.einsum('skgt,tkd->skgd', weights.astype(jnp.bfloat16), value_part.res...]
    all_to_all x2 -> x0, blocking collectives: 54.4 us -> none  [the longest x1 27.7 us: body(): lax.all_to_all(outgoing, 'exp', split_axis=0, concat_axis=0, tiled=True)]
    ppermute x15 -> x0, starting transfers between devices: 28.6 us -> none  [shifted(): lax.ppermute(value, axis, [(source, source + steps) for source in range(f...]
    reduce_scatter x1 -> x0, waiting for transfers between devices: 18.8 us -> none  [body(): lax.psum_scatter(jnp.dot(attended, out_weight, preferred_element_type=jnp...]
    reduce_sum x18 -> x0, other arithmetic: 14.2 us -> none  [the longest x16 13.9 us: update(): weight_sum = weight_sum * shrink + jnp.sum(weights, axis=-1)]
    while x91 -> x0, local copies, waits for them, and re-layouts: 12.6 us -> none
  transfers between devices with their start and end apart: 16 -> 0, of which waited for: 16 -> 0; matrix products, arithmetic and copies ran while one was open for 5% -> 0% of each run, Pallas kernels for 0% -> 0%
where the time goes in v1:
time: 80.6 us; the launch traced here: 79.8 us
  Pallas kernels  75.1 us (93%)
  local copies, waits for them, and re-layouts  4.7 us (6%)
    pallas_call x1, Pallas kernels, fused_body(): pl.pallas_call(layer_kernel, out_shape=jax.ShapeDtypeStruct((tokens, widt...  75.1 us
    unnamed x3, local copies, waits for them, and re-layouts  4.7 us

profile of v1, /device:TPU:24, one launch (start us, length us, event | category | flops | bytes accessed | tf_op | source)
XLA Modules:
  0.0 79.8 jit_solution(5058038847957111575)
XLA Ops:
  0.0 1.4 %copy.12.ids_ref = s32[128,2]{1,0:T(8,128)} copy(s32[128,2]{0,1:T(2,128)} %param.20) | data formatting | bytes 2048 | tf_op args[9]
  1.4 1.4 %copy.13.gw_ref = f32[128,2]{1,0:T(8,128)} copy(f32[128,2]{0,1:T(2,128)} %param.21) | data formatting | bytes 2048 | tf_op args[10]
  2.8 75.1 %shard_map.109 = bf16[128,2048]{1,0:T(8,128)(2,1)} custom-call(bf16[128,2048]{1,0:T(8,128)(2,1)} %hid_ref.1, bf16[256,2048]{1,0:T(8,128)(2,1)} %q_ref.1, bf16[2,128,512]{2,1,0:T(8,128)(2,1)} %bitcast.5, bf16[2,128,512]{2,1,0:T(8,128)(2,1)} %bitcast.6, s32[2,8]{1,0:T(2,128)} %list_ref.1, s32[2,8]{1,0:T(2,128)} %list_ref.1, bf16[2048,2048]{1,0:T(8,128)(2,1)} %wo_ref.1, ...), custom_call_target="tpu_custom_call" | custom-call | flops 14000000000 | bytes 50000000 | tf_op jit(solution)/shard_map/pallas_call | solution.py:502
  77.9 1.9 %copy.15 = bf16[128,2048]{1,0:T(8,128)(2,1)} copy(bf16[128,2048]{1,0:T(8,128)(2,1)} %shard_map.109) | data formatting | bytes 1048576

commit v2 on v1

--- a/solution.py
+++ b/solution.py
@@ -305,7 +305,7 @@
             send(h, across(k), zs.at[h, k], sibling).wait_recv()
             c_send_across(h, k).start()
 
-    for place, (h, k) in enumerate(ORDER):
+    for place, (h, k) in enumerate(ORDER[:-1]):
         if k == 0:
             own[2 * h].wait()
             own[2 * h + 1].wait()
@@ -320,14 +320,13 @@
                 copy.start()
         if place > 0:
             relay_across(*ORDER[place - 1])
-    relay_across(*ORDER[-1])
-    for h in range(2):
+
+    def wait_sibling(h):
         for k in range(4):
             @pl.when(z >= k)
             def _(h=h, k=k):
                 for xx in range(2):
                     send(h, (z - k) * 4 + xx * 2 + 1 - core, zs.at[h, k], sibling).wait_recv()
-    q_copy.wait()
 
     scale = LOG2E / math.sqrt(HD)
     key_row = lax.broadcasted_iota(jnp.int32, (2 * BLK, BLK), 1)
@@ -342,37 +341,34 @@
                 again += jnp.where(listed == list_ref[t : t + 1, i : i + 1], 1.0, 0.0)
             bias_s[t, :, (j - 1) * BLK : j * BLK] = jnp.where(again > 0.0, NEG_FILL, 0.0)
 
-    @pl.loop(0, 2)
-    def _(t):
+    def attend(h, t):
         rows = pl.ds(pl.multiple_of(t * BLK, BLK), BLK)
-        listed = [blk_ref[t, j] for j in range(picks)]
         bias = bias_s[t]
-        for h in range(2):
-            for j in range(picks):
-                kcat[j * BLK : (j + 1) * BLK, :] = kvs[h][listed[j]]
-
-            @pl.loop(0, GROUP // 4)
-            def _(quad):
-                for half in range(2):
-                    first = pl.multiple_of((h * GROUP + quad * 4 + half * 2) * HD, HD)
-                    second = pl.multiple_of((h * GROUP + quad * 4 + half * 2 + 1) * HD, HD)
-                    queries = jnp.concatenate([q_s[rows, pl.ds(first, HD)], q_s[rows, pl.ds(second, HD)]], axis=0)
-                    scores = lax.dot_general(
-                        queries, kcat[:, :HD], (((1,), (1,)), ((), ())), preferred_element_type=jnp.float32
-                    )
-                    near = scores[:, :BLK] * scale + triangle
-                    far = scores[:, BLK:] * scale + bias
-                    top = jnp.maximum(
-                        jnp.max(near, axis=1, keepdims=True), jnp.max(far, axis=1, keepdims=True)
-                    )
-                    near = jnp.exp2(near - top)
-                    far = jnp.exp2(far - top)
-                    total = jnp.sum(near, axis=1, keepdims=True) + jnp.sum(far, axis=1, keepdims=True)
-                    weights = jnp.concatenate([near.astype(jnp.bfloat16), far.astype(jnp.bfloat16)], axis=1)
-                    mixed = jnp.dot(weights, kcat[:, HD:], preferred_element_type=jnp.float32) / total
-                    mixed = mixed.astype(jnp.bfloat16)
-                    att[rows, pl.ds(first, HD)] = mixed[:BLK]
-                    att[rows, pl.ds(second, HD)] = mixed[BLK:]
+        for j in range(picks):
+            kcat[j * BLK : (j + 1) * BLK, :] = kvs[h][blk_ref[t, j]]
+
+        @pl.loop(0, GROUP // 4)
+        def _(quad):
+            for half in range(2):
+                first = pl.multiple_of((h * GROUP + quad * 4 + half * 2) * HD, HD)
+                second = pl.multiple_of((h * GROUP + quad * 4 + half * 2 + 1) * HD, HD)
+                queries = jnp.concatenate([q_s[rows, pl.ds(first, HD)], q_s[rows, pl.ds(second, HD)]], axis=0)
+                scores = lax.dot_general(
+                    queries, kcat[:, :HD], (((1,), (1,)), ((), ())), preferred_element_type=jnp.float32
+                )
+                near = scores[:, :BLK] * scale + triangle
+                far = scores[:, BLK:] * scale + bias
+                top = jnp.maximum(
+                    jnp.max(near, axis=1, keepdims=True), jnp.max(far, axis=1, keepdims=True)
+                )
+                near = jnp.exp2(near - top)
+                far = jnp.exp2(far - top)
+                total = jnp.sum(near, axis=1, keepdims=True) + jnp.sum(far, axis=1, keepdims=True)
+                weights = jnp.concatenate([near.astype(jnp.bfloat16), far.astype(jnp.bfloat16)], axis=1)
+                mixed = jnp.dot(weights, kcat[:, HD:], preferred_element_type=jnp.float32) / total
+                mixed = mixed.astype(jnp.bfloat16)
+                att[rows, pl.ds(first, HD)] = mixed[:BLK]
+                att[rows, pl.ds(second, HD)] = mixed[BLK:]
 
     def chunk(n):
         return pl.ds(pl.multiple_of(n * COLS, COLS), COLS)
@@ -397,18 +393,30 @@
             recv_sem=rr.at[n], device_id=(c, 1 - e), device_id_type=MESH,
         )
 
+    depth = wo_ref.shape[0]
+
+    def project(which):
+        rows = mine if which == 0 else other
+
+        @pl.loop(0, chunks)
+        def _(n):
+            product = jnp.dot(att[rows, :], wbuf[:depth, chunk(n)], preferred_element_type=jnp.float32)
+            part_s[rows, chunk(n)] = product.astype(jnp.bfloat16)
+            part_send(which, n).start()
+
+    wait_sibling(0)
+    q_copy.wait()
+    attend(0, e)
+    relay(*ORDER[-1])
+    relay_across(*ORDER[-2])
+    attend(0, 1 - e)
+    relay_across(*ORDER[-1])
+    wait_sibling(1)
+    attend(1, e)
     wo_copy.wait()
-    depth = wo_ref.shape[0]
-
-    @pl.loop(0, chunks)
-    def _(n):
-        product = jnp.dot(att[...], wbuf[:depth, chunk(n)], preferred_element_type=jnp.float32)
-        part_s[:, chunk(n)] = product.astype(jnp.bfloat16)
-        part_send(0, n).start()
-
-    @pl.loop(0, chunks)
-    def _(n):
-        part_send(1, n).start()
+    project(0)
+    attend(1, 1 - e)
+    project(1)
 
     wd_copy.start()
     hid_copy.wait()

time: 80.6 us -> 76.9 us (0.954)
  Pallas kernels: 75.1 us -> 71.9 us
    pallas_call x1, Pallas kernels: 75.1 us -> 71.9 us  [fused_body(): pl.pallas_call(layer_kernel, out_shape=jax.ShapeDtypeStruct((tokens, widt...]
where the time goes in v2:
time: 76.9 us; the launch traced here: 76.6 us
  Pallas kernels  71.9 us (93%)
  local copies, waits for them, and re-layouts  4.7 us (6%)
    pallas_call x1, Pallas kernels, fused_body(): pl.pallas_call(layer_kernel, out_shape=jax.ShapeDtypeStruct((tokens, widt...  71.9 us
    unnamed x3, local copies, waits for them, and re-layouts  4.7 us

profile of v2, /device:TPU:24, one launch (start us, length us, event | category | flops | bytes accessed | tf_op | source)
XLA Modules:
  0.0 76.6 jit_solution(16798567249918482257)
XLA Ops:
  0.0 1.4 %copy.12.ids_ref = s32[128,2]{1,0:T(8,128)} copy(s32[128,2]{0,1:T(2,128)} %param.20) | data formatting | bytes 2048 | tf_op args[9]
  1.4 1.4 %copy.13.gw_ref = f32[128,2]{1,0:T(8,128)} copy(f32[128,2]{0,1:T(2,128)} %param.21) | data formatting | bytes 2048 | tf_op args[10]
  2.8 71.9 %shard_map.109 = bf16[128,2048]{1,0:T(8,128)(2,1)} custom-call(bf16[128,2048]{1,0:T(8,128)(2,1)} %hid_ref.1, bf16[256,2048]{1,0:T(8,128)(2,1)} %q_ref.1, bf16[2,128,512]{2,1,0:T(8,128)(2,1)} %bitcast.5, bf16[2,128,512]{2,1,0:T(8,128)(2,1)} %bitcast.6, s32[2,8]{1,0:T(2,128)} %list_ref.1, s32[2,8]{1,0:T(2,128)} %list_ref.1, bf16[2048,2048]{1,0:T(8,128)(2,1)} %wo_ref.1, ...), custom_call_target="tpu_custom_call" | custom-call | flops 14000000000 | bytes 50000000 | tf_op jit(solution)/shard_map/pallas_call | solution.py:510
  74.8 1.9 %copy.15 = bf16[128,2048]{1,0:T(8,128)(2,1)} copy(bf16[128,2048]{1,0:T(8,128)(2,1)} %shard_map.109) | data formatting | bytes 1048576

commit v3 on v2

--- a/solution.py
+++ b/solution.py
@@ -376,20 +376,20 @@
     def part_send(which, n):
         rows = mine if which == 0 else other
         return pltpu.make_async_remote_copy(
-            src_ref=part_s.at[rows, chunk(n)], dst_ref=part_r.at[rows, chunk(n)], send_sem=ps.at[which, n],
+            src_ref=part_s.at[n, rows], dst_ref=part_r.at[n, rows], send_sem=ps.at[which, n],
             recv_sem=pr.at[which, n], device_id=(c, 1 - e), device_id_type=MESH,
         )
 
     def part_recv(which, n):
         rows = other if which == 0 else mine
         return pltpu.make_async_remote_copy(
-            src_ref=part_s.at[rows, chunk(n)], dst_ref=part_r.at[rows, chunk(n)], send_sem=ps.at[which, n],
+            src_ref=part_s.at[n, rows], dst_ref=part_r.at[n, rows], send_sem=ps.at[which, n],
             recv_sem=pr.at[which, n], device_id=(c, 1 - e), device_id_type=MESH,
         )
 
     def ret_send(n):
         return pltpu.make_async_remote_copy(
-            src_ref=ret_s.at[:, chunk(n)], dst_ref=ret_r.at[:, chunk(n)], send_sem=rs.at[n],
+            src_ref=ret_s.at[n], dst_ref=ret_r.at[n], send_sem=rs.at[n],
             recv_sem=rr.at[n], device_id=(c, 1 - e), device_id_type=MESH,
         )
 
@@ -401,7 +401,7 @@
         @pl.loop(0, chunks)
         def _(n):
             product = jnp.dot(att[rows, :], wbuf[:depth, chunk(n)], preferred_element_type=jnp.float32)
-            part_s[rows, chunk(n)] = product.astype(jnp.bfloat16)
+            part_s[n, rows, :] = product.astype(jnp.bfloat16)
             part_send(which, n).start()
 
     wait_sibling(0)
@@ -434,7 +434,13 @@
 
         hidden = (
             hid_s[rows, :].astype(jnp.float32)
-            + (part_s[rows, :].astype(jnp.float32) + part_r[rows, :].astype(jnp.float32))
+            + jnp.concatenate(
+                [
+                    part_s[n, rows, :].astype(jnp.float32) + part_r[n, rows, :].astype(jnp.float32)
+                    for n in range(chunks)
+                ],
+                axis=1,
+            )
         ).astype(jnp.bfloat16)
         hid_s[rows, :] = hidden
         hidden_f = hidden.astype(jnp.float32)
@@ -469,11 +475,11 @@
                     preferred_element_type=jnp.float32,
                 )
             if turn == 0:
-                ret_s[:, chunk(n)] = total.astype(jnp.bfloat16)
+                ret_s[n] = total.astype(jnp.bfloat16)
                 ret_send(n).start()
             else:
                 ret_send(n).wait_recv()
-                total += ret_r[:, chunk(n)].astype(jnp.float32)
+                total += ret_r[n].astype(jnp.float32)
                 out_ref[:, chunk(n)] = (hid_s[rows, chunk(n)].astype(jnp.float32) + total).astype(jnp.bfloat16)
 
     @pl.loop(0, chunks)
@@ -521,13 +527,13 @@
             pltpu.VMEM(queries.shape, bf16),
             pltpu.VMEM((experts * FF, width), bf16),
             pltpu.VMEM(w_gate_up.shape, bf16),
-            pltpu.VMEM((2 * tokens, width), bf16),
-            pltpu.VMEM((2 * tokens, width), bf16),
+            pltpu.VMEM((chunks, 2 * tokens, COLS), bf16),
+            pltpu.VMEM((chunks, 2 * tokens, COLS), bf16),
             pltpu.VMEM((2 * tokens, width), bf16),
             pltpu.VMEM((tokens, width), bf16),
             pltpu.VMEM((tokens, experts * FF), bf16),
-            pltpu.VMEM((tokens, width), bf16),
-            pltpu.VMEM((tokens, width), bf16),
+            pltpu.VMEM((chunks, tokens, COLS), bf16),
+            pltpu.VMEM((chunks, tokens, COLS), bf16),
             pltpu.VMEM((2 * tokens, HD), jnp.float32),
             dma((4,)), dma((4,)), dma((4,)),
             dma((2, 4)), dma((2, 4)), dma((2, 8)), dma((2, 16)),

time: 76.9 us -> 76.9 us (level)
  no operation moved by 1% of the time
where the time goes in v3:
time: 76.9 us; the launch traced here: 76.6 us
  Pallas kernels  71.9 us (93%)
  local copies, waits for them, and re-layouts  4.7 us (6%)
    pallas_call x1, Pallas kernels, fused_body(): pl.pallas_call(layer_kernel, out_shape=jax.ShapeDtypeStruct((tokens, widt...  71.9 us
    unnamed x3, local copies, waits for them, and re-layouts  4.7 us

profile of v3, /device:TPU:24, one launch (start us, length us, event | category | flops | bytes accessed | tf_op | source)
XLA Modules:
  0.0 76.6 jit_solution(11172746197144706996)
XLA Ops:
  0.0 1.4 %copy.12.ids_ref = s32[128,2]{1,0:T(8,128)} copy(s32[128,2]{0,1:T(2,128)} %param.20) | data formatting | bytes 2048 | tf_op args[9]
  1.4 1.4 %copy.13.gw_ref = f32[128,2]{1,0:T(8,128)} copy(f32[128,2]{0,1:T(2,128)} %param.21) | data formatting | bytes 2048 | tf_op args[10]
  2.8 71.9 %shard_map.109 = bf16[128,2048]{1,0:T(8,128)(2,1)} custom-call(bf16[128,2048]{1,0:T(8,128)(2,1)} %hid_ref.1, bf16[256,2048]{1,0:T(8,128)(2,1)} %q_ref.1, bf16[2,128,512]{2,1,0:T(8,128)(2,1)} %bitcast.5, bf16[2,128,512]{2,1,0:T(8,128)(2,1)} %bitcast.6, s32[2,8]{1,0:T(2,128)} %list_ref.1, s32[2,8]{1,0:T(2,128)} %list_ref.1, bf16[2048,2048]{1,0:T(8,128)(2,1)} %wo_ref.1, ...), custom_call_target="tpu_custom_call" | custom-call | flops 14000000000 | bytes 50000000 | tf_op jit(solution)/shard_map/pallas_call | solution.py:516
  74.8 1.9 %copy.15 = bf16[128,2048]{1,0:T(8,128)(2,1)} copy(bf16[128,2048]{1,0:T(8,128)(2,1)} %shard_map.109) | data formatting | bytes 1048576
